TPU v7x, 32 devices: a whole 2x2x4 slice. The times are simulated.
32 devices in a mesh: groups: 2 (over y), seq: 4 (over z), tensor: 2 (over x), sub: 2 (over core).
Axes of the slice: x: 2, y: 2, z: 4, core: 2. Of those that a mesh axis runs over, the one named last changes fastest.
Arguments:
- layer_input: bfloat16 [3072, 8192], P(('groups', 'seq'), ('tensor', 'sub')), parts along dimension 0, may hold values from -6 to 6
- out_grad: bfloat16 [3072, 2, 1024], P(('groups', 'seq')), parts along dimension 0, may hold values from -6 to 6
- base_weight: bfloat16 [2048, 8192], P('seq', ('tensor', 'sub')), may hold values from -0.125 to 0.125
- adapter_mid: bfloat16 [3072, 128], P(('groups', 'seq')), parts along dimension 0, may hold values from -0.29882812 to 0.29882812
- adapter_down: bfloat16 [16, 8192, 128], P(('groups', 'seq'), ('tensor', 'sub')), parts along dimension 0, may hold values from -0.75 to 0.75
- adapter_up: bfloat16 [16, 2, 64, 1024], P(('groups', 'seq'), None, None, ('tensor', 'sub')), parts along dimension 0, may hold values from -0.005859375 to 0.005859375
- tenant_counts: int32 [16], P('groups'), parts along dimension 0, may hold values from 1 to 384, as said below
- seg_starts: int32 [16], P('groups'), parts along dimension 0, may hold values from 0 to 1408, as said below
- owner_slot: int32 [16], P('groups'), parts along dimension 0, may hold values from 0 to 7, as said below
Outputs:
- grad_input: bfloat16 [3072, 8192], P(('groups', 'seq'), ('tensor', 'sub')), parts along dimension 0
- grad_down: bfloat16 [16, 8192, 128], P(('groups', 'seq'), ('tensor', 'sub')), parts along dimension 0
- up_adapter_gradient: bfloat16 [16, 2, 64, 1024], P(('groups', 'seq'), None, None, ('tensor', 'sub')), parts along dimension 0
There are 2 independent parts, one for each index of `groups`. A program takes and returns all parts, laid end to end along the dimension named above; an argument that names none is the same for every part. Nothing has to cross between parts.
Inputs may be any that keep to these rules, and one draw needn't show every extreme that they name: Tenants lie in the batch in the order 0 to 7; each segment is a whole number of blocks of 128 rows, ceil(tenant_counts[t] / 128) of them, and only its first tenant_counts[t] rows are live; the busiest tenant has 384 live rows (3 full blocks), and no tenant has more. seg_starts[0] = 0; seg_starts rises by the segments' padded lengths, and the last segment ends at row 1536. owner_slot is owner_slot is a permutation; tenant t's rows of the adapter arrays and gradients are row owner_slot[t], held by seq index owner_slot[t] // 2; that index depends only on t mod (4) and differs between different values of it, and owner_slot[t] mod 2 = t // 4.
All inputs are finite; a program needn't handle non-finite values.
Results may differ from a plain program's by a relative error of at most 0.0049.
Values may be sent and summed in bfloat16 or wider, within the bound.
A program may use at most 128 MiB of HBM per device.

v0:
```python
import jax
import jax.numpy as jnp
from jax import lax
from jax.sharding import PartitionSpec as P

BLK = 128


adapter_scale_factor = 2.0


def tenant_tables(tenant_counts, seg_starts, owner_slot, blocks):
    tenant_ids = jnp.arange(owner_slot.shape[0], dtype=jnp.int32)
    block_first = jnp.arange(blocks, dtype=jnp.int32) * BLK
    block_tenant = (
        jnp.sum((seg_starts[None, :] <= block_first[:, None]).astype(jnp.int32), axis=1) - 1
    )
    tenant_hit = block_tenant[:, None] == tenant_ids[None, :]

    def per_block(values):
        return jnp.sum(jnp.where(tenant_hit, values[None, :], 0), axis=1)

    return (
        block_first,
        block_tenant,
        per_block(seg_starts),
        per_block(tenant_counts),
        per_block(owner_slot),
    )


def local(
    layer_input,
    out_grad,
    base_weight,
    adapter_mid,
    adapter_down,
    adapter_up,
    tenant_counts,
    seg_starts,
    owner_slot,
):
    highest_precision_mode = lax.Precision.HIGHEST
    seq_count = lax.axis_size("seq")
    my_index = lax.axis_index("seq")
    shard_index = lax.axis_index(("tensor", "sub"))
    tok_rows, width_local = layer_input.shape
    ten_dev = adapter_down.shape[0]
    rank_width = adapter_down.shape[2]
    kv_local = adapter_up.shape[3]
    kv_total = out_grad.shape[2]
    blk_dev = tok_rows // BLK
    blocks = blk_dev * seq_count
    piece_cols = width_local // seq_count
    tenants = owner_slot.shape[0]
    tenant_ids = jnp.arange(tenants, dtype=jnp.int32)
    block_first, block_tenant, start_all, count_all, slot_all = tenant_tables(
        tenant_counts, seg_starts, owner_slot, blocks
    )
    my_first = lax.dynamic_slice_in_dim(block_first, my_index * blk_dev, blk_dev)
    my_start = lax.dynamic_slice_in_dim(start_all, my_index * blk_dev, blk_dev)
    my_count = lax.dynamic_slice_in_dim(count_all, my_index * blk_dev, blk_dev)
    my_slot = lax.dynamic_slice_in_dim(slot_all, my_index * blk_dev, blk_dev)
    offsets = my_first[:, None] + jnp.arange(BLK, dtype=jnp.int32)[None, :] - my_start[:, None]
    live_rows = offsets < my_count[:, None]
    masked = jnp.where(live_rows.reshape(tok_rows, 1, 1), out_grad, jnp.zeros_like(out_grad))
    masked_flat = masked.reshape(tok_rows, 2 * kv_total)
    masked_own = lax.dynamic_slice_in_dim(masked, shard_index * kv_local, kv_local, 2)
    gradient_block_list = masked_own.reshape(blk_dev, BLK, 2, kv_local)
    weight_full, up_all = (
        lax.all_gather(base_weight, "seq", axis=0, tiled=True),
        lax.all_gather(adapter_up, "seq", axis=0, tiled=True),
    )
    base_term = jnp.dot(masked_flat, weight_full, preferred_element_type=jnp.float32)
    own_select = (my_slot[:, None] == tenant_ids[None, :]).astype(jnp.bfloat16)
    up_projection_blocks = jnp.einsum(
        "bt,tjrk->bjrk", own_select, up_all, preferred_element_type=jnp.float32
    ).astype(jnp.bfloat16)
    low_part = jnp.einsum(
        "zpex,zehx->zpeh",
        gradient_block_list,
        up_projection_blocks,
        preferred_element_type=jnp.float32,
    ).reshape(tok_rows, rank_width)
    reduced_rank_sum = lax.psum(low_part, ("tensor", "sub"))
    reduced_rank_mine = (adapter_scale_factor * reduced_rank_sum).astype(jnp.bfloat16)
    lowrank_all = lax.all_gather(reduced_rank_mine, "seq", axis=0, tiled=True)
    mid_blocks = adapter_mid.reshape(blk_dev, BLK, 2, rank_width // 2)
    up_projection_share = adapter_scale_factor * jnp.einsum(
        "bqjr,bqjk->bjrk", mid_blocks, gradient_block_list, preferred_element_type=jnp.float32
    )
    block_select = (my_slot[:, None] == tenant_ids[None, :]).astype(jnp.float32)
    up_grad = lax.psum_scatter(
        jnp.einsum(
            "on,olqp->nlqp", block_select, up_projection_share, precision=highest_precision_mode
        ),
        "seq",
        scatter_dimension=0,
        tiled=True,
    )
    up_adapter_gradient = up_grad.astype(jnp.bfloat16)
    input_cols = layer_input.reshape(tok_rows, seq_count, piece_cols)
    down_cols = adapter_down.reshape(ten_dev, seq_count, piece_cols, rank_width)
    feat_rows, down_feat = (
        lax.all_to_all(input_cols, "seq", split_axis=1, concat_axis=0, tiled=True),
        lax.all_to_all(down_cols, "seq", split_axis=1, concat_axis=0, tiled=True),
    )
    feat_blocks = feat_rows.reshape(blocks, BLK, piece_cols)
    down_feat = down_feat.reshape(tenants, piece_cols, rank_width)
    low_blocks = lowrank_all.reshape(blocks, BLK, rank_width)
    adapter_slot_choice = slot_all[:, None] == tenant_ids[None, :]
    down_projection_share = jnp.einsum(
        "bqc,bqr->bcr", feat_blocks, low_blocks, preferred_element_type=jnp.float32
    )
    down_grad = jnp.einsum(
        "bt,bcr->tcr",
        adapter_slot_choice.astype(jnp.float32),
        down_projection_share,
        precision=highest_precision_mode,
    ).astype(jnp.bfloat16)
    down_projection_blocks = jnp.einsum(
        "bt,tcr->bcr",
        adapter_slot_choice.astype(jnp.bfloat16),
        down_feat,
        preferred_element_type=jnp.float32,
    ).astype(jnp.bfloat16)
    side_feat = jnp.einsum(
        "bqr,bcr->bqc", low_blocks, down_projection_blocks, preferred_element_type=jnp.float32
    ).astype(jnp.bfloat16)
    grad_down, adapter_side_term = (
        lax.all_to_all(
            down_grad.reshape(seq_count, ten_dev, piece_cols, rank_width),
            "seq",
            split_axis=0,
            concat_axis=2,
            tiled=True,
        ),
        lax.all_to_all(
            side_feat.reshape(seq_count, tok_rows, piece_cols),
            "seq",
            split_axis=0,
            concat_axis=2,
            tiled=True,
        ),
    )
    grad_input = (
        base_term + adapter_side_term.reshape(tok_rows, width_local).astype(jnp.float32)
    ).astype(jnp.bfloat16)
    return (grad_input, grad_down.reshape(ten_dev, width_local, rank_width), up_adapter_gradient)


def solution(mesh):
    return jax.shard_map(
        local,
        mesh=mesh,
        in_specs=(
            P(("groups", "seq"), ("tensor", "sub")),
            P(("groups", "seq"), None, None),
            P("seq", ("tensor", "sub")),
            P(("groups", "seq"), None),
            P(("groups", "seq"), ("tensor", "sub"), None),
            P(("groups", "seq"), None, None, ("tensor", "sub")),
            P("groups"),
            P("groups"),
            P("groups"),
        ),
        out_specs=(
            P(("groups", "seq"), ("tensor", "sub")),
            P(("groups", "seq"), ("tensor", "sub"), None),
            P(("groups", "seq"), None, None, ("tensor", "sub")),
        ),
        check_vma=False,
    )
```

profile of v0, /device:TPU:24, one launch (start us, length us, event | category | flops | bytes accessed | tf_op | source)
XLA Modules:
  0.0 333.3 jit_solution(13078992325162195858)
XLA Ops:
  8.0 0.0 all-reduce.2.cloned.1.call-start
  8.1 0.7 convert_reduce_fusion
  8.8 0.1 dynamic_slice.15
  8.9 0.8 select_reduce_fusion
  9.7 0.1 dynamic_slice.16
  9.7 0.1 dynamic_slice.17
  9.8 3.7 %copy.66 = bf16[384,2,1024]{0,2,1:T(8,128)(2,1)S(1)} copy(bf16[384,2,1024]{2,1,0:T(2,128)(2,1)} %param.10) | data formatting | bytes 3145728 | tf_op args[1]
  13.6 0.1 fusion.15
  13.6 0.0 copy-start.3
  13.6 0.2 broadcast_select_fusion
  13.8 0.0 copy-start
  13.8 0.1 constant_dynamic-slice_fusion
  13.9 0.0 copy-start.4
  13.9 0.2 copy.68
  14.1 0.1 dynamic_slice.18
  14.1 0.4 copy-done.3
  14.5 16.4 %all_gather.10 = bf16[8,2,64,256]{3,2,1,0:T(8,128)(2,1)S(1)} all-gather(bf16[2,2,64,256]{3,2,1,0:T(8,128)(2,1)S(1)} %copy-done.3), channel_id=1, replica_groups=mesh['groups'=2,'seq'=4,'tensor'=2,'sub'=2] {'seq'}, dimensions={0}, use_global_device_ids=true | all-gather | bytes 655360 | tf_op jit(solution)/shard_map/all_gather | solution.py:72
  31.0 0.4 convolution_convert_fusion.3
  31.4 0.3 convolution_bitcast_fusion.1
  31.6 0.1 copy.71
  31.8 0.0 copy-done
  31.8 0.7 copy.111
  32.5 0.0 all-reduce.2.cloned.1.call-update
  32.5 0.0 reduce-scatter.2.cloned.1.call-start
  32.6 0.0 copy-done.4
  32.6 0.1 reshape.113
  32.7 0.3 fusion.1
  33.0 0.9 fusion.3
  33.9 1.3 copy.86
  35.2 0.0 copy-start.2
  35.2 0.0 reduce-scatter.2.cloned.1.call-update
  35.2 0.0 all-gather.2.cloned.1.call-start
  35.3 0.5 all-gather.2.cloned.1.call-update
  35.8 0.6 copy-done.2
  36.4 0.0 copy-start.1
  36.5 1.0 copy.73
  37.5 5.1 %all-to-all-start = ((bf16[2,4,512,128]{3,2,0,1:T(8,128)(2,1)}), bf16[2,4,512,128]{3,2,0,1:T(8,128)(2,1)S(1)}, u32[]{:S(2)}, u32[]{:S(2)}) async-start(bf16[2,4,512,128]{3,2,0,1:T(8,128)(2,1)} %copy.73), calls=%async_computation | async-start | bytes 2097152 | tf_op jit(solution)/shard_map/all_to_all | solution.py:106
  42.6 0.0 copy-done.1
  42.6 1.6 copy.77
  44.2 35.5 %all-to-all-done = bf16[2,4,512,128]{3,2,0,1:T(8,128)(2,1)S(1)} async-done(((bf16[2,4,512,128]{3,2,0,1:T(8,128)(2,1)}), bf16[2,4,512,128]{3,2,0,1:T(8,128)(2,1)S(1)}, u32[]{:S(2)}, u32[]{:S(2)}) %all-to-all-start) | async-done | bytes 1048608 | tf_op jit(solution)/shard_map/all_to_all | solution.py:106
  79.7 5.9 %all-to-all-start.2 = ((bf16[384,4,512]{0,2,1:T(8,128)(2,1)}), bf16[384,4,512]{0,2,1:T(8,128)(2,1)S(1)}, u32[]{:S(2)}, u32[]{:S(2)}) async-start(bf16[384,4,512]{0,2,1:T(8,128)(2,1)} %bitcast.15), calls=%async_computation.2 | async-start | bytes 3145728 | tf_op jit(solution)/shard_map/all_to_all | solution.py:105
  85.6 0.0 all-reduce.2.cloned.1.call-done
  85.6 0.9 multiply_convert_fusion
  86.6 100.7 %all_gather.11 = bf16[1536,128]{0,1:T(8,128)(2,1)S(1)} all-gather(bf16[384,128]{0,1:T(8,128)(2,1)S(1)} %multiply_convert_fusion), channel_id=1, replica_groups=mesh['groups'=2,'seq'=4,'tensor'=2,'sub'=2] {'seq'}, dimensions={0}, use_global_device_ids=true | all-gather | bytes 491520 | tf_op jit(solution)/shard_map/all_gather | solution.py:87
  187.3 0.2 copy.72
  187.5 1.0 convolution_convert_fusion
  188.5 1.9 convolution_convert_fusion.1
  190.4 0.0 all-to-all-done.2
  190.4 5.1 %all-to-all-start.1 = ((bf16[4,384,512]{2,1,0:T(8,128)(2,1)}), bf16[4,384,512]{2,1,0:T(8,128)(2,1)}, u32[]{:S(2)}, u32[]{:S(2)}) async-start(bf16[4,384,512]{2,1,0:T(8,128)(2,1)} %bitcast.12), calls=%async_computation.1 | async-start | bytes 3145728 | tf_op jit(solution)/shard_map/all_to_all | solution.py:138
  195.5 1.7 copy.78
  197.2 2.1 convolution_bitcast_fusion
  199.2 3.6 %copy.80 = f32[12,512,128]{2,0,1:T(8,128)} copy(f32[12,512,128]{1,2,0:T(8,128)S(1)} %convolution_bitcast_fusion) | data formatting | bytes 6291456 | tf_op jit(solution)/shard_map/bqc,bqr->bcr/dot_general | solution.py:112
  202.8 3.8 %convolution_convert_fusion.2 = bf16[8,512,128]{2,0,1:T(8,128)(2,1)S(1)} fusion(f32[12,512,128]{2,0,1:T(8,128)} %copy.80, s32[12]{0:T(128)S(1)} %get-tuple-element.18), kind=kOutput, calls=%fused_computation.7 | convolution fusion | flops 76021856 | bytes 4194352 | tf_op jit(solution)/shard_map/bt,bcr->tcr/dot_general | solution.py:115
  206.6 1.7 copy.81
  208.3 62.1 %all-to-all-done.1 = bf16[4,384,512]{2,1,0:T(8,128)(2,1)} async-done(((bf16[4,384,512]{2,1,0:T(8,128)(2,1)}), bf16[4,384,512]{2,1,0:T(8,128)(2,1)}, u32[]{:S(2)}, u32[]{:S(2)}) %all-to-all-start.1) | async-done | bytes 1572896 | tf_op jit(solution)/shard_map/all_to_all | solution.py:138
  270.3 5.1 %all-to-all-start.3 = ((bf16[4,2,512,128]{3,1,2,0:T(2,128)(2,1)}), bf16[4,2,512,128]{3,1,2,0:T(2,128)(2,1)}, u32[]{:S(2)}, u32[]{:S(2)}) async-start(bf16[4,2,512,128]{3,1,2,0:T(2,128)(2,1)} %copy.81), calls=%async_computation.3 | async-start | bytes 2097152 | tf_op jit(solution)/shard_map/all_to_all | solution.py:131
  275.4 1.6 convert_element_type.51
  277.0 1.8 convert_bitcast_fusion
  278.9 2.0 copy.76
  280.9 1.4 copy.93
  282.3 25.0 %all-to-all-done.3 = bf16[4,2,512,128]{3,1,2,0:T(2,128)(2,1)} async-done(((bf16[4,2,512,128]{3,1,2,0:T(2,128)(2,1)}), bf16[4,2,512,128]{3,1,2,0:T(2,128)(2,1)}, u32[]{:S(2)}, u32[]{:S(2)}) %all-to-all-start.3) | async-done | bytes 1048608 | tf_op jit(solution)/shard_map/all_to_all | solution.py:131
  307.3 2.3 copy.87
  309.7 7.7 %all-gather.2.cloned.1.call-done = bf16[2048,2048]{1,0:T(8,128)(2,1)} async-done(((bf16[512,2048]{1,0:T(8,128)(2,1)}), bf16[2048,2048]{1,0:T(8,128)(2,1)}) %all-gather.2.cloned.1.call-update) | async-done | bytes 8388624 | tf_op jit(solution)/shard_map/all_gather | solution.py:71
  317.4 8.5 %add_convert_fusion = bf16[384,2048]{1,0:T(8,128)(2,1)} fusion(f32[384,2048]{1,0:T(8,128)S(1)} %bitcast.60, bf16[384,2048]{0,1:T(8,128)(2,1)} %bitcast.62, bf16[2048,2048]{1,0:T(8,128)(2,1)} %all-gather.2.cloned.1.call-done), kind=kOutput, calls=%fused_computation.1 | convolution fusion | flops 3222798336 | bytes 14680064 | tf_op jit(solution)/shard_map/dot_general | solution.py:74
  (3 shorter events, 0.0 us)
Async XLA Ops:
  8.0 77.6 %all-reduce.2.cloned.1.call-start = ((), (), s32[]{:S(2)}) async-start(), calls=%async_computation.6 | async-start | bytes 393216 | tf_op jit(solution)/shard_map/psum | solution.py:85
  13.6 0.9 copy-start.3
  13.8 18.0 %copy-start = (bf16[384,2,1024]{0,2,1:T(8,128)(2,1)}, bf16[384,2,1024]{0,2,1:T(8,128)(2,1)S(1)}, u32[]{:S(2)}) copy-start(bf16[384,2,1024]{0,2,1:T(8,128)(2,1)S(1)} %broadcast_select_fusion) | copy-start | bytes 4718596
  13.9 18.7 %copy-start.4 = (bf16[384,128]{1,0:T(8,128)(2,1)S(1)}, bf16[384,128]{1,0:T(8,128)(2,1)}, u32[]{:S(2)}) copy-start(bf16[384,128]{1,0:T(8,128)(2,1)} %param.12) | copy-start | bytes 294916
  32.5 242.9 %reduce-scatter.2.cloned.1.call-start = ((), (), s32[]{:S(2)}) async-start(), calls=%async_computation.7 | async-start | bytes 1310720 | tf_op jit(solution)/shard_map/reduce_scatter | solution.py:93
  35.2 1.2 copy-start.2
  35.2 282.1 %all-gather.2.cloned.1.call-start = ((), (), s32[]{:S(2)}) async-start(), calls=%async_computation.5 | async-start | bytes 10485760 | tf_op jit(solution)/shard_map/all_gather | solution.py:71
  36.4 6.1 %copy-start.1 = (bf16[384,2048]{1,0:T(8,128)(2,1)S(1)}, bf16[384,2048]{1,0:T(8,128)(2,1)}, u32[]{:S(2)}) copy-start(bf16[384,2048]{1,0:T(8,128)(2,1)} %param.9) | copy-start | bytes 4718596
  37.5 42.2 %all-to-all-start = ((bf16[2,4,512,128]{3,2,0,1:T(8,128)(2,1)}), bf16[2,4,512,128]{3,2,0,1:T(8,128)(2,1)S(1)}, u32[]{:S(2)}, u32[]{:S(2)}) async-start(bf16[2,4,512,128]{3,2,0,1:T(8,128)(2,1)} %copy.73), calls=%async_computation | async-start | bytes 2097152 | tf_op jit(solution)/shard_map/all_to_all | solution.py:106
  79.7 110.7 %all-to-all-start.2 = ((bf16[384,4,512]{0,2,1:T(8,128)(2,1)}), bf16[384,4,512]{0,2,1:T(8,128)(2,1)S(1)}, u32[]{:S(2)}, u32[]{:S(2)}) async-start(bf16[384,4,512]{0,2,1:T(8,128)(2,1)} %bitcast.15), calls=%async_computation.2 | async-start | bytes 3145728 | tf_op jit(solution)/shard_map/all_to_all | solution.py:105
  190.4 79.9 %all-to-all-start.1 = ((bf16[4,384,512]{2,1,0:T(8,128)(2,1)}), bf16[4,384,512]{2,1,0:T(8,128)(2,1)}, u32[]{:S(2)}, u32[]{:S(2)}) async-start(bf16[4,384,512]{2,1,0:T(8,128)(2,1)} %bitcast.12), calls=%async_computation.1 | async-start | bytes 3145728 | tf_op jit(solution)/shard_map/all_to_all | solution.py:138
  270.3 37.0 %all-to-all-start.3 = ((bf16[4,2,512,128]{3,1,2,0:T(2,128)(2,1)}), bf16[4,2,512,128]{3,1,2,0:T(2,128)(2,1)}, u32[]{:S(2)}, u32[]{:S(2)}) async-start(bf16[4,2,512,128]{3,1,2,0:T(2,128)(2,1)} %copy.81), calls=%async_computation.3 | async-start | bytes 2097152 | tf_op jit(solution)/shard_map/all_to_all | solution.py:131
Sparse Core Ops, SparseCore 0:
  32.6 32.7 all-reduce.1
Sparse Core Ops, SparseCore 1:
  35.4 42.1 reduce-scatter.1
  79.0 238.4 all-gather.1
where the time goes:
time: 338 us; the launch traced here: 333 us
  waiting for transfers between devices  131 us (39%)
  blocking collectives  117 us (35%)
  local copies, waits for them, and re-layouts  23.1 us (7%)
  starting transfers between devices  21.3 us (6%)
  matrix products  19.1 us (6%)
  between operations  15.7 us (5%)
  other arithmetic  6.15 us (2%)
    all_gather x1, blocking collectives, local(): lowrank_all = lax.all_gather(reduced_rank_mine, 'seq', axis=0, tiled=True)  101 us
    all_to_all x1, waiting for transfers between devices, local(): lax.all_to_all(side_feat.reshape(seq_count, tok_rows, piece_cols), 'seq',...  62.1 us
    all_to_all x1, waiting for transfers between devices, local(): lax.all_to_all(down_cols, 'seq', split_axis=1, concat_axis=0, tiled=True)  35.5 us
    all_to_all x1, waiting for transfers between devices, local(): lax.all_to_all(down_grad.reshape(seq_count, ten_dev, piece_cols, rank_wid...  25 us
    all_gather x1, blocking collectives, local(): lax.all_gather(adapter_up, 'seq', axis=0, tiled=True)  16.4 us
    unnamed x15, local copies, waits for them, and re-layouts  10.8 us
    dot_general x1, matrix products, local(): jnp.dot(masked_flat, weight_full, preferred_element_type=jnp.float32)  8.5 us
    all_gather x1, waiting for transfers between devices, local(): lax.all_gather(base_weight, 'seq', axis=0, tiled=True)  7.74 us
  transfers between devices with their start and end apart: 7, of which 4 were waited for; matrix products, arithmetic and copies ran while one was open for 9% of the time, Pallas kernels for 0%

commit v1 on v0

--- a/solution.py
+++ b/solution.py
@@ -1,6 +1,10 @@
+import functools
+
 import jax
 import jax.numpy as jnp
 from jax import lax
+from jax.experimental import pallas as pl
+from jax.experimental.pallas import tpu as pltpu
 from jax.sharding import PartitionSpec as P
 
 BLK = 128
@@ -149,9 +153,405 @@
     return (grad_input, grad_down.reshape(ten_dev, width_local, rank_width), up_adapter_gradient)
 
 
+MESH = pl.DeviceIdType.MESH
+CHUNKS = 2
+F32 = jnp.float32
+BF16 = jnp.bfloat16
+
+
+def hosting(planes, tok_blocks):
+    blocks, tenants = planes * tok_blocks, planes * 2
+    low, high = [], []
+    for s in range(planes):
+        first, last = s * tok_blocks, (s + 1) * tok_blocks - 1
+        least = max(first // tok_blocks, first - (blocks - tenants))
+        most = min(last, tenants - 1 - (blocks - 1 - last) // tok_blocks)
+        if least < planes:
+            low.append(s)
+        if most >= planes:
+            high.append(s)
+    return max(low), min(high)
+
+
+def line_kernel(
+    S, T, C,
+    counts, starts, owners,
+    x, og, mid, w_hbm, dn_hbm, up_hbm,
+    gi, gd, gu,
+    w, dn, up, low, gown, gright, gleft, uown, uright, uleft, masked, lsel, msel,
+    copy_sem, up_s, up_r, low_s, low_r,
+    w_s, w_r, y_s, y_r, dn_s, dn_r, g_s, g_r, u_s, u_r,
+):
+    s = lax.axis_index("seq")
+    g = lax.axis_index("groups")
+    t = lax.axis_index("tensor")
+    c = lax.axis_index("sub")
+    M = T * C
+    m = t * C + c
+    rows, width = x.shape
+    depth = w_hbm.shape[0]
+    half = depth // 2
+    piece = half // CHUNKS
+    kv_local = up_hbm.shape[3]
+    kv = kv_local * M
+    nblk = rows // BLK
+    N = 2 * S
+    rank2 = mid.shape[1]
+    rank = rank2 // 2
+    last0, first1 = hosting(S, nblk)
+    right, left = {"seq": s + 1}, {"seq": s - 1}
+
+    def partners():
+        for k in range(1, M):
+            q = lax.rem(m + k, M)
+            yield k, {"tensor": q // C, "sub": lax.rem(q, C)}
+
+    def remote(src, dst, send, recv, dev):
+        return pltpu.make_async_remote_copy(
+            src_ref=src, dst_ref=dst, send_sem=send, recv_sem=recv, device_id=dev, device_id_type=MESH
+        )
+
+    own = (
+        pltpu.make_async_copy(w_hbm, w.at[pl.ds(s * depth, depth)], copy_sem.at[0]),
+        pltpu.make_async_copy(dn_hbm, dn.at[pl.ds(2 * s, 2)], copy_sem.at[1]),
+        pltpu.make_async_copy(up_hbm, up.at[pl.ds(2 * s, 2)], copy_sem.at[2]),
+    )
+    for cp in own:
+        cp.start()
+
+    barrier = pltpu.get_barrier_semaphore()
+    for k in range(1, S):
+        pl.semaphore_signal(barrier, inc=1, device_id={"seq": lax.rem(s + k, S)}, device_id_type=MESH)
+    pl.semaphore_signal(barrier, inc=1, device_id={"groups": 1 - g}, device_id_type=MESH)
+    for _, dev in partners():
+        pl.semaphore_signal(barrier, inc=1, device_id=dev, device_id_type=MESH)
+    pl.semaphore_wait(barrier, S - 1 + 1 + M - 1)
+    for cp in own:
+        cp.wait()
+
+    def up_copy(k, plane, target):
+        part = up.at[pl.ds(2 * plane, 2)]
+        return remote(part, part, up_s.at[k - 1], up_r.at[k - 1], {"seq": target})
+
+    for k in range(1, S):
+        up_copy(k, s, lax.rem(s + k, S)).start()
+
+    def w_rows(plane, hlf, i):
+        return w.at[pl.ds(pl.multiple_of(plane * depth + hlf * half + i * piece, 16), piece)]
+
+    def origin(way, k):
+        return s - k if way == 0 else s + k
+
+    def held(plane):
+        return jnp.logical_and(plane >= 0, plane < S)
+
+    def w_copy(way, k, plane, i):
+        part = w_rows(plane, g, i)
+        return remote(part, part, w_s.at[way, k - 1, i], w_r.at[way, k - 1, i], left if way else right)
+
+    def y_copy(way, k, plane, i, hlf):
+        part = w_rows(plane, hlf, i)
+        return remote(part, part, y_s.at[way, k - 1, i], y_r.at[way, k - 1, i], {"groups": 1 - g})
+
+    def dn_copy(way, k, plane, j):
+        part = dn.at[2 * plane + j]
+        return remote(part, part, dn_s.at[way, k - 1, j], dn_r.at[way, k - 1, j], left if way else right)
+
+    def can_send(way, k, j=None):
+        plane = origin(way, k - 1)
+        nxt = s - 1 if way else s + 1
+        ok = jnp.logical_and(held(plane), held(nxt))
+        if j == 0:
+            ok = jnp.logical_and(ok, nxt <= last0)
+        if j == 1:
+            ok = jnp.logical_and(ok, nxt >= first1)
+        return ok
+
+    def can_recv(way, k, j=None):
+        ok = held(origin(way, k))
+        if j == 0:
+            ok = jnp.logical_and(ok, s <= last0)
+        if j == 1:
+            ok = jnp.logical_and(ok, s >= first1)
+        return ok
+
+    def send_w(k, way, i):
+        @pl.when(can_send(way, k))
+        def _():
+            w_copy(way, k, origin(way, k - 1), i).start()
+
+    def send_dn(k, way, j):
+        @pl.when(can_send(way, k, j))
+        def _():
+            dn_copy(way, k, origin(way, k - 1), j).start()
+
+    for i in range(CHUNKS):
+        for way in range(2):
+            send_w(1, way, i)
+    for j in range(2):
+        for way in range(2):
+            send_dn(1, way, j)
+
+    for p in range(S):
+        for j in range(2):
+            unused = s > last0 if j == 0 else s < first1
+
+            @pl.when(jnp.logical_and(unused, s != p))
+            def _(p=p, j=j):
+                dn[2 * p + j] = jnp.zeros(dn.shape[1:], dn.dtype)
+
+    slots = []
+    for b in range(nblk):
+        first = (s * nblk + b) * BLK
+        tenant = jnp.int32(-1)
+        for n in range(N):
+            tenant = tenant + jnp.where(starts[n] <= first, 1, 0).astype(jnp.int32)
+        live = counts[tenant] - (first - starts[tenant])
+        slots.append(owners[tenant])
+        here = pl.ds(b * BLK, BLK)
+        keep = lax.broadcasted_iota(jnp.int32, (BLK, 2 * kv), 0) < live
+        value = og[here, :].astype(F32)
+        masked[here, :] = jnp.where(keep, value, 0.0).astype(BF16)
+
+    def own_features(j):
+        return pl.ds(pl.multiple_of(j * kv + m * kv_local, 128), kv_local)
+
+    for k in range(1, S):
+        up_copy(k, lax.rem(s + S - k, S), s).wait_recv()
+    for b in range(nblk):
+        here = pl.ds(b * BLK, BLK)
+        for j in range(2):
+            low[m, here, j * rank : (j + 1) * rank] = lax.dot_general(
+                masked[here, own_features(j)],
+                up[slots[b], j],
+                (((1,), (1,)), ((), ())),
+                preferred_element_type=F32,
+            )
+
+    def low_copy(k, index, dev):
+        return remote(low.at[index], low.at[index], low_s.at[k - 1], low_r.at[k - 1], dev)
+
+    for k, dev in partners():
+        low_copy(k, m, dev).start()
+
+    for b in range(nblk):
+        here = pl.ds(b * BLK, BLK)
+        value = mid[here, :].astype(F32)
+        for n in range(N):
+            hit = jnp.where(slots[b] == n, 1.0, 0.0).astype(F32)
+            msel[here, n * rank2 : (n + 1) * rank2] = (value * hit).astype(BF16)
+    for n in range(N):
+        both = msel[:, n * rank2 : (n + 1) * rank2]
+        for j in range(2):
+            share = lax.dot_general(
+                both, masked[:, own_features(j)], (((0,), (0,)), ((), ())), preferred_element_type=F32
+            )
+            uown[n, j] = (adapter_scale_factor * share[j * rank : (j + 1) * rank, :]).astype(BF16)
+
+    for k, dev in partners():
+        low_copy(k, lax.rem(m + M - k, M), dev).wait_recv()
+    total = low[0]
+    for q in range(1, M):
+        total = total + low[q]
+    lowrank = (adapter_scale_factor * total).astype(BF16).astype(F32)
+    for b in range(nblk):
+        here = pl.ds(b * BLK, BLK)
+        value = lowrank[b * BLK : (b + 1) * BLK, :]
+        for n in range(N):
+            hit = jnp.where(slots[b] == n, 1.0, 0.0).astype(F32)
+            lsel[here, n * rank2 : (n + 1) * rank2] = (value * hit).astype(BF16)
+
+    step = 256
+
+    @pl.loop(0, width // step)
+    def _(i):
+        at = pl.ds(pl.multiple_of(i * step, step), step)
+        share = lax.dot_general(
+            x[:, at], lsel[...], (((0,), (0,)), ((), ())), preferred_element_type=F32
+        )
+        for n in range(N):
+            gown[n, at, :] = share[:, n * rank2 : (n + 1) * rank2].astype(BF16)
+
+    g_in, u_in = (gright, gleft), (uright, uleft)
+
+    def grad_copies(way, d, j):
+        n = 2 * d + j
+        dev = left if way else right
+        return (
+            remote(gown.at[n], g_in[way].at[n], g_s.at[n], g_r.at[way, n], dev),
+            remote(uown.at[n], u_in[way].at[n], u_s.at[n], u_r.at[way, n], dev),
+        )
+
+    def gives(way, plane, j):
+        if way == 0:
+            return plane >= (0 if j == 0 else first1)
+        return plane <= (last0 if j == 0 else S - 1)
+
+    def add_in(way, n):
+        @pl.loop(0, width // step)
+        def _(i):
+            at = pl.ds(pl.multiple_of(i * step, step), step)
+            gown[n, at, :] = (gown[n, at, :].astype(F32) + g_in[way][n, at, :].astype(F32)).astype(BF16)
+
+        uown[n] = (uown[n].astype(F32) + u_in[way][n].astype(F32)).astype(BF16)
+
+    def grad_step(way, plane):
+        @pl.when(s == plane)
+        def _():
+            behind = plane + 1 if way else plane - 1
+            dests = range(plane, -1, -1) if way else range(plane, S)
+            for d in reversed(dests):
+                for j in range(2):
+                    if 0 <= behind < S and gives(way, behind, j):
+                        for cp in grad_copies(way, d, j):
+                            cp.wait_recv()
+                        add_in(way, 2 * d + j)
+                    if d != plane and gives(way, plane, j):
+                        for cp in grad_copies(way, d, j):
+                            cp.start()
+
+    grad_step(0, 0)
+    grad_step(1, S - 1)
+    for k in range(1, S):
+        for i in range(CHUNKS):
+            for way in range(2):
+
+                @pl.when(can_recv(way, k))
+                def _(way=way, i=i):
+                    w_copy(way, k, origin(way, k), i).wait_recv()
+                    y_copy(way, k, origin(way, k), i, g).start()
+
+                if k < S - 1:
+                    send_w(k + 1, way, i)
+        for j in range(2):
+            for way in range(2):
+
+                @pl.when(can_recv(way, k, j))
+                def _(way=way, j=j):
+                    dn_copy(way, k, origin(way, k), j).wait_recv()
+
+                if k < S - 1:
+                    send_dn(k + 1, way, j)
+        grad_step(0, k)
+        grad_step(1, S - 1 - k)
+
+    gd[...] = gown[pl.ds(2 * s, 2)]
+    gu[...] = uown[pl.ds(2 * s, 2)]
+
+    for k in range(1, S):
+        for i in range(CHUNKS):
+            for way in range(2):
+
+                @pl.when(can_recv(way, k))
+                def _(way=way, i=i, k=k):
+                    y_copy(way, k, origin(way, k), i, 1 - g).wait_recv()
+
+    @pl.loop(0, width // step)
+    def _(i):
+        at = pl.ds(pl.multiple_of(i * step, step), step)
+        base = jnp.dot(masked[...], w[:, at], preferred_element_type=F32)
+        side = jnp.zeros((rows, step), F32)
+        for n in range(N):
+            side = side + lax.dot_general(
+                lsel[:, n * rank2 : (n + 1) * rank2],
+                dn[n, at, :],
+                (((1,), (1,)), ((), ())),
+                preferred_element_type=F32,
+            )
+        gi[:, at] = (base + side.astype(BF16).astype(F32)).astype(BF16)
+
+    for k in range(1, S):
+        up_copy(k, s, lax.rem(s + k, S)).wait_send()
+    for k, dev in partners():
+        low_copy(k, m, dev).wait_send()
+    for k in range(1, S):
+        for way in range(2):
+            for i in range(CHUNKS):
+
+                @pl.when(can_send(way, k))
+                def _(k=k, way=way, i=i):
+                    w_copy(way, k, origin(way, k - 1), i).wait_send()
+
+                @pl.when(can_recv(way, k))
+                def _(k=k, way=way, i=i):
+                    y_copy(way, k, origin(way, k), i, g).wait_send()
+
+            for j in range(2):
+
+                @pl.when(can_send(way, k, j))
+                def _(k=k, way=way, j=j):
+                    dn_copy(way, k, origin(way, k - 1), j).wait_send()
+
+    for plane in range(S):
+
+        @pl.when(s == plane)
+        def _(plane=plane):
+            for d in range(S):
+                for j in range(2):
+                    way = 0 if d > plane else 1
+                    if d != plane and gives(way, plane, j):
+                        for cp in grad_copies(way, d, j):
+                            cp.wait_send()
+
+
+def line_local(S, T, C, layer_input, out_grad, base_weight, adapter_mid, adapter_down, adapter_up,
+               tenant_counts, seg_starts, owner_slot):
+    rows, width = layer_input.shape
+    N, M = 2 * S, T * C
+    rank2 = adapter_down.shape[2]
+    kv2 = 2 * out_grad.shape[2]
+    up_shape = adapter_up.shape[1:]
+    vmem = pl.BlockSpec(memory_space=pltpu.VMEM)
+    smem = pl.BlockSpec(memory_space=pltpu.SMEM)
+    hbm = pl.BlockSpec(memory_space=pl.ANY)
+    dma = pltpu.SemaphoreType.DMA
+    grads = pltpu.VMEM((N, width, rank2), BF16)
+    ups = pltpu.VMEM((N,) + up_shape, BF16)
+    return pl.pallas_call(
+        functools.partial(line_kernel, S, T, C),
+        out_shape=(
+            jax.ShapeDtypeStruct((rows, width), BF16),
+            jax.ShapeDtypeStruct(adapter_down.shape, BF16),
+            jax.ShapeDtypeStruct(adapter_up.shape, BF16),
+        ),
+        in_specs=[smem] * 3 + [vmem] * 3 + [hbm] * 3,
+        out_specs=(vmem, vmem, vmem),
+        scratch_shapes=[
+            pltpu.VMEM((S * base_weight.shape[0], width), BF16),
+            grads,
+            ups,
+            pltpu.VMEM((M, rows, rank2), F32),
+            grads, grads, grads,
+            ups, ups, ups,
+            pltpu.VMEM((rows, kv2), BF16),
+            pltpu.VMEM((rows, N * rank2), BF16),
+            pltpu.VMEM((rows, N * rank2), BF16),
+            dma((3,)),
+            dma((S - 1,)), dma((S - 1,)),
+            dma((M - 1,)), dma((M - 1,)),
+            dma((2, S - 1, CHUNKS)), dma((2, S - 1, CHUNKS)),
+            dma((2, S - 1, CHUNKS)), dma((2, S - 1, CHUNKS)),
+            dma((2, S - 1, 2)), dma((2, S - 1, 2)),
+            dma((N,)), dma((2, N)),
+            dma((N,)), dma((2, N)),
+        ],
+        compiler_params=pltpu.CompilerParams(
+            collective_id=0, has_side_effects=True, vmem_limit_bytes=58 * 1024 * 1024
+        ),
+        name="line",
+    )(
+        tenant_counts, seg_starts, owner_slot,
+        layer_input, out_grad.reshape(rows, kv2), adapter_mid, base_weight, adapter_down, adapter_up,
+    )
+
+
 def solution(mesh):
+    S, T, C = mesh.shape["seq"], mesh.shape["tensor"], mesh.shape["sub"]
+    short = 2 <= S <= 4 and mesh.shape["groups"] == 2
+    body = functools.partial(line_local, S, T, C) if short else local
+
     return jax.shard_map(
-        local,
+        body,
         mesh=mesh,
         in_specs=(
             P(("groups", "seq"), ("tensor", "sub")),

time: 338 us -> 179 us (0.53)
  Pallas kernels: 0 us -> 168 us
  waiting for transfers between devices: 131 us -> 0 us
  blocking collectives: 117 us -> 0 us
  starting transfers between devices: 21.3 us -> 0 us
  matrix products: 19.1 us -> 0 us
  local copies, waits for them, and re-layouts: 23.1 us -> 7.49 us
  between operations: 15.7 us -> 0.65 us
  other arithmetic: 6.15 us -> 0 us
    pallas_call x0 -> x1, Pallas kernels: none -> 168 us  [line_local(): pl.pallas_call(functools.partial(line_kernel, S, T, C), out_shape=(jax.Sh...]
    all_to_all x4 -> x0, waiting for transfers between devices: 123 us -> none  [the longest x1 62.1 us: local(): lax.all_to_all(side_feat.reshape(seq_count, tok_rows, piece_cols), 'seq',...]
    all_gather x2 -> x0, blocking collectives: 117 us -> none  [the longest x1 101 us: local(): lowrank_all = lax.all_gather(reduced_rank_mine, 'seq', axis=0, tiled=True)]
    all_to_all x4 -> x0, starting transfers between devices: 21.2 us -> none  [the longest x1 5.9 us: local(): lax.all_to_all(input_cols, 'seq', split_axis=1, concat_axis=0, tiled=True)]
    dot_general x9 -> x0, matrix products: 19.1 us -> none  [the longest x1 8.5 us: local(): jnp.dot(masked_flat, weight_full, preferred_element_type=jnp.float32)]
    all_gather x1 -> x0, waiting for transfers between devices: 7.74 us -> none  [local(): lax.all_gather(base_weight, 'seq', axis=0, tiled=True)]
    dot_general x2 -> x0, local copies, waits for them, and re-layouts: 4.87 us -> none  [the longest x1 3.56 us: local(): jnp.einsum('bqc,bqr->bcr', feat_blocks, low_blocks, preferred_element_typ...]
    convert_element_type x3 -> x0, other arithmetic: 4.39 us -> none  [the longest x1 1.83 us: local(): adapter_side_term.reshape(tok_rows, width_local).astype(jnp.float32)]
  transfers between devices with their start and end apart: 7 -> 0, of which waited for: 4 -> 0; matrix products, arithmetic and copies ran while one was open for 9% -> 0% of each run, Pallas kernels for 0% -> 0%
where the time goes in v1:
time: 179 us; the launch traced here: 176 us
  Pallas kernels  168 us (94%)
  local copies, waits for them, and re-layouts  7.49 us (4%)
    pallas_call x1, Pallas kernels, line_local(): pl.pallas_call(functools.partial(line_kernel, S, T, C), out_shape=(jax.Sh...  168 us
    unnamed x8, local copies, waits for them, and re-layouts  7.49 us

profile of v1, /device:TPU:24, one launch (start us, length us, event | category | flops | bytes accessed | tf_op | source)
XLA Modules:
  0.0 176.4 jit_solution(6344207359707337573)
XLA Ops:
  0.6 3.0 %copy.12 = bf16[48,8,2,1024]{3,1,2,0:T(8,128)(2,1)} copy(bf16[48,8,2,1024]{3,2,1,0:T(2,128)(2,1)} %bitcast.3) | data formatting | bytes 3145728
  3.6 168.2 %line.1 = (bf16[384,2048]{1,0:T(8,128)(2,1)}, bf16[2,2048,128]{2,1,0:T(8,128)(2,1)}, bf16[2,2,64,256]{3,2,1,0:T(8,128)(2,1)}) custom-call(s32[8]{0:T(128)} %counts.1, s32[8]{0:T(128)} %starts.1, s32[8]{0:T(128)} %owners.1, bf16[384,2048]{1,0:T(8,128)(2,1)} %x.1, bf16[384,2048]{1,0:T(8,128)(2,1)} %bitcast.2, bf16[384,128]{1,0:T(8,128)(2,1)} %mid.1, ...), custom_call_target="tpu_custom_call" | custom-call | tf_op jit(solution)/shard_map/line/pallas_call | solution.py:510
  171.9 0.0 copy-start
  171.9 2.8 %copy.16 = bf16[384,2048]{1,0:T(8,128)(2,1)} copy(bf16[384,2048]{1,0:T(8,128)(2,1)} %get-tuple-element.6) | data formatting | bytes 3145728
  174.7 0.0 copy-done
  174.7 0.0 copy-start.1
  174.7 1.0 copy.17
  175.7 0.1 copy-done.1
  175.7 0.7 copy.18
Async XLA Ops:
  171.9 2.8 %copy-start = (bf16[2,2048,128]{2,1,0:T(8,128)(2,1)S(1)}, bf16[2,2048,128]{2,1,0:T(8,128)(2,1)}, u32[]{:S(2)}) copy-start(bf16[2,2048,128]{2,1,0:T(8,128)(2,1)} %get-tuple-element.7) | copy-start | bytes 3145732
  174.7 1.0 copy-start.1

commit v2 on v1

--- a/solution.py
+++ b/solution.py
@@ -178,7 +178,7 @@
     counts, starts, owners,
     x, og, mid, w_hbm, dn_hbm, up_hbm,
     gi, gd, gu,
-    w, dn, up, low, gown, gright, gleft, uown, uright, uleft, masked, lsel, msel,
+    w, dn, up, low, gown, gright, gleft, mix, uown, uright, uleft, masked, lsel, msel,
     copy_sem, up_s, up_r, low_s, low_r,
     w_s, w_r, y_s, y_r, dn_s, dn_r, g_s, g_r, u_s, u_r,
 ):
@@ -201,10 +201,10 @@
     last0, first1 = hosting(S, nblk)
     right, left = {"seq": s + 1}, {"seq": s - 1}
 
-    def partners():
-        for k in range(1, M):
-            q = lax.rem(m + k, M)
-            yield k, {"tensor": q // C, "sub": lax.rem(q, C)}
+    def stage(axis):
+        size, index = (C, c) if axis == "sub" else (T, t)
+        for k in range(1, size):
+            yield k, {axis: lax.rem(index + k, size)}, lax.rem(index + size - k, size)
 
     def remote(src, dst, send, recv, dev):
         return pltpu.make_async_remote_copy(
@@ -223,18 +223,38 @@
     for k in range(1, S):
         pl.semaphore_signal(barrier, inc=1, device_id={"seq": lax.rem(s + k, S)}, device_id_type=MESH)
     pl.semaphore_signal(barrier, inc=1, device_id={"groups": 1 - g}, device_id_type=MESH)
-    for _, dev in partners():
-        pl.semaphore_signal(barrier, inc=1, device_id=dev, device_id_type=MESH)
-    pl.semaphore_wait(barrier, S - 1 + 1 + M - 1)
+    for axis in ("sub", "tensor"):
+        for _, dev, _ in stage(axis):
+            pl.semaphore_signal(barrier, inc=1, device_id=dev, device_id_type=MESH)
+    pl.semaphore_wait(barrier, S - 1 + 1 + C - 1 + T - 1)
     for cp in own:
         cp.wait()
 
-    def up_copy(k, plane, target):
-        part = up.at[pl.ds(2 * plane, 2)]
-        return remote(part, part, up_s.at[k - 1], up_r.at[k - 1], {"seq": target})
-
-    for k in range(1, S):
-        up_copy(k, s, lax.rem(s + k, S)).start()
+    def up_copy(k, plane, target, j):
+        part = up.at[2 * plane + j]
+        return remote(part, part, up_s.at[k - 1, j], up_r.at[k - 1, j], {"seq": target})
+
+    def wants(plane, j):
+        return plane <= last0 if j == 0 else plane >= first1
+
+    def ups(act):
+        for k in range(1, S):
+            for j in range(2):
+                ahead, behind = lax.rem(s + k, S), lax.rem(s + S - k, S)
+                if act == "recv":
+
+                    @pl.when(wants(s, j))
+                    def _(k=k, j=j, behind=behind):
+                        up_copy(k, behind, s, j).wait_recv()
+
+                else:
+
+                    @pl.when(wants(ahead, j))
+                    def _(k=k, j=j, ahead=ahead):
+                        cp = up_copy(k, s, ahead, j)
+                        cp.start() if act == "start" else cp.wait_send()
+
+    ups("start")
 
     def w_rows(plane, hlf, i):
         return w.at[pl.ds(pl.multiple_of(plane * depth + hlf * half + i * piece, 16), piece)]
@@ -280,10 +300,60 @@
         def _():
             w_copy(way, k, origin(way, k - 1), i).start()
 
+    cut = (S // 2 - 1, S // 2)
+
+    def tenant_of(block):
+        index = jnp.int32(-1)
+        for n in range(N):
+            index = index + jnp.where(starts[n] <= block * BLK, 1, 0).astype(jnp.int32)
+        return index
+
+    takes_grads = (tenant_of(S // 2 * nblk - 1) >= S, tenant_of(S // 2 * nblk) < S)
+
+    def mix_copy(k, way):
+        to = dn.at[2 * origin(way, k - 1) + way]
+        dev = left if way else right
+        return remote(mix.at[way, k - 1], to, dn_s.at[way, k - 1, way], dn_r.at[way, k - 1, way], dev)
+
+    def dn_sends(k, way, j, act):
+        ok = can_send(way, k, j)
+        if j == way:
+
+            @pl.when(jnp.logical_and(ok, s == cut[way]))
+            def _():
+                if act == "wait":
+                    mix_copy(k, way).wait_send()
+
+            ok = jnp.logical_and(ok, s != cut[way])
+
+        @pl.when(ok)
+        def _():
+            cp = dn_copy(way, k, origin(way, k - 1), j)
+            cp.wait_send() if act == "wait" else cp.start()
+
     def send_dn(k, way, j):
-        @pl.when(can_send(way, k, j))
+        dn_sends(k, way, j, "start")
+
+    def mixed_dest(way, k):
+        return k - 1 if way else S - k
+
+    def mixed(way, plane, j):
+        return plane == cut[way] and j != way
+
+    def send_mix(k, way):
+        @pl.when(s == cut[way])
         def _():
-            dn_copy(way, k, origin(way, k - 1), j).start()
+            hit = jnp.where(takes_grads[way], 1.0, 0.0).astype(F32)
+            own_map = 2 * origin(way, k - 1) + way
+            n = 2 * mixed_dest(way, k) + 1 - way
+
+            @pl.loop(0, width // 256)
+            def _(i):
+                at = pl.ds(pl.multiple_of(i * 256, 256), 256)
+                value = gown[n, at, :].astype(F32) * hit + dn[own_map, at, :].astype(F32) * (1.0 - hit)
+                mix[way, k - 1, at, :] = value.astype(BF16)
+
+            mix_copy(k, way).start()
 
     for i in range(CHUNKS):
         for way in range(2):
@@ -309,30 +379,40 @@
         live = counts[tenant] - (first - starts[tenant])
         slots.append(owners[tenant])
         here = pl.ds(b * BLK, BLK)
-        keep = lax.broadcasted_iota(jnp.int32, (BLK, 2 * kv), 0) < live
-        value = og[here, :].astype(F32)
-        masked[here, :] = jnp.where(keep, value, 0.0).astype(BF16)
+        keep = lax.broadcasted_iota(jnp.int32, (BLK, kv), 0) < live
+        for j in range(2):
+            value = og[here, j, :].astype(F32)
+            masked[here, j * kv : (j + 1) * kv] = jnp.where(keep, value, 0.0).astype(BF16)
 
     def own_features(j):
         return pl.ds(pl.multiple_of(j * kv + m * kv_local, 128), kv_local)
 
-    for k in range(1, S):
-        up_copy(k, lax.rem(s + S - k, S), s).wait_recv()
+    ups("recv")
     for b in range(nblk):
         here = pl.ds(b * BLK, BLK)
         for j in range(2):
-            low[m, here, j * rank : (j + 1) * rank] = lax.dot_general(
+            low[c, here, j * rank : (j + 1) * rank] = lax.dot_general(
                 masked[here, own_features(j)],
                 up[slots[b], j],
                 (((1,), (1,)), ((), ())),
                 preferred_element_type=F32,
             )
 
-    def low_copy(k, index, dev):
-        return remote(low.at[index], low.at[index], low_s.at[k - 1], low_r.at[k - 1], dev)
-
-    for k, dev in partners():
-        low_copy(k, m, dev).start()
+    def low_copy(k, index, dev, first):
+        return remote(
+            low.at[first + index], low.at[first + index], low_s.at[first + k - 1], low_r.at[first + k - 1], dev
+        )
+
+    for k, dev, _ in stage("sub"):
+        low_copy(k, c, dev, 0).start()
+    for k, dev, behind in stage("sub"):
+        low_copy(k, behind, dev, 0).wait_recv()
+    chip_sum = low[0]
+    for q in range(1, C):
+        chip_sum = chip_sum + low[q]
+    low[C + t] = chip_sum
+    for k, dev, _ in stage("tensor"):
+        low_copy(k, t, dev, C).start()
 
     for b in range(nblk):
         here = pl.ds(b * BLK, BLK)
@@ -348,11 +428,11 @@
             )
             uown[n, j] = (adapter_scale_factor * share[j * rank : (j + 1) * rank, :]).astype(BF16)
 
-    for k, dev in partners():
-        low_copy(k, lax.rem(m + M - k, M), dev).wait_recv()
-    total = low[0]
-    for q in range(1, M):
-        total = total + low[q]
+    for k, dev, behind in stage("tensor"):
+        low_copy(k, behind, dev, C).wait_recv()
+    total = low[C]
+    for q in range(1, T):
+        total = total + low[C + q]
     lowrank = (adapter_scale_factor * total).astype(BF16).astype(F32)
     for b in range(nblk):
         here = pl.ds(b * BLK, BLK)
@@ -361,6 +441,35 @@
             hit = jnp.where(slots[b] == n, 1.0, 0.0).astype(F32)
             lsel[here, n * rank2 : (n + 1) * rank2] = (value * hit).astype(BF16)
 
+    def hop_w(k):
+        for i in range(CHUNKS):
+            for way in range(2):
+
+                @pl.when(can_recv(way, k))
+                def _(way=way, i=i):
+                    w_copy(way, k, origin(way, k), i).wait_recv()
+                    if k < S - 1:
+                        send_w(k + 1, way, i)
+                    y_copy(way, k, origin(way, k), i, g).start()
+
+    def hop_dn(k):
+        for j in range(2):
+            for way in range(2):
+
+                @pl.when(can_recv(way, k, j))
+                def _(way=way, j=j):
+                    dn_copy(way, k, origin(way, k), j).wait_recv()
+                    if k < S - 1:
+                        send_dn(k + 1, way, j)
+
+                if j == way and k < S // 2:
+                    send_mix(k + 1, way)
+
+    def hop(k):
+        hop_w(k)
+        hop_dn(k)
+
+    hop_w(1)
     step = 256
 
     @pl.loop(0, width // step)
@@ -374,69 +483,79 @@
 
     g_in, u_in = (gright, gleft), (uright, uleft)
 
-    def grad_copies(way, d, j):
+    def grad_copies(way, sender, d, j):
         n = 2 * d + j
         dev = left if way else right
-        return (
-            remote(gown.at[n], g_in[way].at[n], g_s.at[n], g_r.at[way, n], dev),
-            remote(uown.at[n], u_in[way].at[n], u_s.at[n], u_r.at[way, n], dev),
-        )
+        small = remote(uown.at[n], u_in[way].at[n], u_s.at[n], u_r.at[way, n], dev)
+        if mixed(way, sender, j):
+            return (small,)
+        return (remote(gown.at[n], g_in[way].at[n], g_s.at[n], g_r.at[way, n], dev), small)
 
     def gives(way, plane, j):
         if way == 0:
             return plane >= (0 if j == 0 else first1)
         return plane <= (last0 if j == 0 else S - 1)
 
-    def add_in(way, n):
+    def add_in(way, sender, d, j):
+        n = 2 * d + j
+        came, scale = g_in[way].at[n], None
+        if mixed(way, sender, j):
+            k = d + 1 if way else S - d
+            came = dn.at[2 * (sender + k - 1 if way else sender - k + 1) + way]
+            scale = jnp.where(takes_grads[way], 1.0, 0.0).astype(F32)
+
         @pl.loop(0, width // step)
         def _(i):
             at = pl.ds(pl.multiple_of(i * step, step), step)
-            gown[n, at, :] = (gown[n, at, :].astype(F32) + g_in[way][n, at, :].astype(F32)).astype(BF16)
+            value = came[at, :].astype(F32)
+            if scale is not None:
+                value = value * scale
+            gown[n, at, :] = (gown[n, at, :].astype(F32) + value).astype(BF16)
 
         uown[n] = (uown[n].astype(F32) + u_in[way][n].astype(F32)).astype(BF16)
 
-    def grad_step(way, plane):
+    def grad_turn(way, plane, alone):
         @pl.when(s == plane)
         def _():
             behind = plane + 1 if way else plane - 1
-            dests = range(plane, -1, -1) if way else range(plane, S)
+            dests = range(plane - 1, -1, -1) if way else range(plane + 1, S)
             for d in reversed(dests):
                 for j in range(2):
+                    joined = 0 <= behind < S and gives(way, behind, j)
+                    if joined != alone and gives(way, plane, j):
+                        if joined:
+                            for cp in grad_copies(way, behind, d, j):
+                                cp.wait_recv()
+                            add_in(way, behind, d, j)
+                        for cp in grad_copies(way, plane, d, j):
+                            cp.start()
+
+    def grad_end(plane):
+        @pl.when(s == plane)
+        def _():
+            for way in range(2):
+                behind = plane + 1 if way else plane - 1
+                for j in range(2):
                     if 0 <= behind < S and gives(way, behind, j):
-                        for cp in grad_copies(way, d, j):
+                        for cp in grad_copies(way, behind, plane, j):
                             cp.wait_recv()
-                        add_in(way, 2 * d + j)
-                    if d != plane and gives(way, plane, j):
-                        for cp in grad_copies(way, d, j):
-                            cp.start()
-
-    grad_step(0, 0)
-    grad_step(1, S - 1)
-    for k in range(1, S):
-        for i in range(CHUNKS):
-            for way in range(2):
-
-                @pl.when(can_recv(way, k))
-                def _(way=way, i=i):
-                    w_copy(way, k, origin(way, k), i).wait_recv()
-                    y_copy(way, k, origin(way, k), i, g).start()
-
-                if k < S - 1:
-                    send_w(k + 1, way, i)
-        for j in range(2):
-            for way in range(2):
-
-                @pl.when(can_recv(way, k, j))
-                def _(way=way, j=j):
-                    dn_copy(way, k, origin(way, k), j).wait_recv()
-
-                if k < S - 1:
-                    send_dn(k + 1, way, j)
-        grad_step(0, k)
-        grad_step(1, S - 1 - k)
-
-    gd[...] = gown[pl.ds(2 * s, 2)]
-    gu[...] = uown[pl.ds(2 * s, 2)]
+                        add_in(way, behind, plane, j)
+
+    for way in range(2):
+        send_mix(1, way)
+    grad_turn(0, 0, True)
+    grad_turn(1, S - 1, True)
+    hop_dn(1)
+    for p in range(1, S - 1):
+        grad_turn(0, p, True)
+        grad_turn(1, S - 1 - p, True)
+    for k in range(2, S - 1):
+        hop(k)
+    for p in range(1, S - 1):
+        grad_turn(0, p, False)
+        grad_turn(1, S - 1 - p, False)
+    if S > 2:
+        hop(S - 1)
 
     for k in range(1, S):
         for i in range(CHUNKS):
@@ -460,10 +579,16 @@
             )
         gi[:, at] = (base + side.astype(BF16).astype(F32)).astype(BF16)
 
-    for k in range(1, S):
-        up_copy(k, s, lax.rem(s + k, S)).wait_send()
-    for k, dev in partners():
-        low_copy(k, m, dev).wait_send()
+    for p in range(S):
+        grad_end(p)
+    gd[...] = gown[pl.ds(2 * s, 2)]
+    gu[...] = uown[pl.ds(2 * s, 2)]
+
+    ups("wait")
+    for k, dev, _ in stage("sub"):
+        low_copy(k, c, dev, 0).wait_send()
+    for k, dev, _ in stage("tensor"):
+        low_copy(k, t, dev, C).wait_send()
     for k in range(1, S):
         for way in range(2):
             for i in range(CHUNKS):
@@ -478,9 +603,7 @@
 
             for j in range(2):
 
-                @pl.when(can_send(way, k, j))
-                def _(k=k, way=way, j=j):
-                    dn_copy(way, k, origin(way, k - 1), j).wait_send()
+                dn_sends(k, way, j, "wait")
 
     for plane in range(S):
 
@@ -490,14 +613,14 @@
                 for j in range(2):
                     way = 0 if d > plane else 1
                     if d != plane and gives(way, plane, j):
-                        for cp in grad_copies(way, d, j):
+                        for cp in grad_copies(way, plane, d, j):
                             cp.wait_send()
 
 
 def line_local(S, T, C, layer_input, out_grad, base_weight, adapter_mid, adapter_down, adapter_up,
                tenant_counts, seg_starts, owner_slot):
     rows, width = layer_input.shape
-    N, M = 2 * S, T * C
+    N = 2 * S
     rank2 = adapter_down.shape[2]
     kv2 = 2 * out_grad.shape[2]
     up_shape = adapter_up.shape[1:]
@@ -520,15 +643,16 @@
             pltpu.VMEM((S * base_weight.shape[0], width), BF16),
             grads,
             ups,
-            pltpu.VMEM((M, rows, rank2), F32),
+            pltpu.VMEM((C + T, rows, rank2), F32),
             grads, grads, grads,
+            pltpu.VMEM((2, S // 2, width, rank2), BF16),
             ups, ups, ups,
             pltpu.VMEM((rows, kv2), BF16),
             pltpu.VMEM((rows, N * rank2), BF16),
             pltpu.VMEM((rows, N * rank2), BF16),
             dma((3,)),
-            dma((S - 1,)), dma((S - 1,)),
-            dma((M - 1,)), dma((M - 1,)),
+            dma((S - 1, 2)), dma((S - 1, 2)),
+            dma((C + T,)), dma((C + T,)),
             dma((2, S - 1, CHUNKS)), dma((2, S - 1, CHUNKS)),
             dma((2, S - 1, CHUNKS)), dma((2, S - 1, CHUNKS)),
             dma((2, S - 1, 2)), dma((2, S - 1, 2)),
@@ -541,13 +665,13 @@
         name="line",
     )(
         tenant_counts, seg_starts, owner_slot,
-        layer_input, out_grad.reshape(rows, kv2), adapter_mid, base_weight, adapter_down, adapter_up,
+        layer_input, out_grad, adapter_mid, base_weight, adapter_down, adapter_up,
     )
 
 
 def solution(mesh):
     S, T, C = mesh.shape["seq"], mesh.shape["tensor"], mesh.shape["sub"]
-    short = 2 <= S <= 4 and mesh.shape["groups"] == 2
+    short = S == 4 and mesh.shape["groups"] == 2
     body = functools.partial(line_local, S, T, C) if short else local
 
     return jax.shard_map(

time: 179 us -> 160 us (0.89); the launches traced: 176 us -> 160 us
  Pallas kernels: 168 us -> 155 us
  local copies, waits for them, and re-layouts: 7.49 us -> 4.5 us
    pallas_call x1, Pallas kernels: 168 us -> 155 us  [line_local(): pl.pallas_call(functools.partial(line_kernel, S, T, C), out_shape=(jax.Sh...]
    unnamed x8 -> x7, local copies, waits for them, and re-layouts: 7.49 us -> 4.5 us
where the time goes in v2:
time: 160 us
  Pallas kernels  155 us (97%)
  local copies, waits for them, and re-layouts  4.5 us (3%)
    pallas_call x1, Pallas kernels, line_local(): pl.pallas_call(functools.partial(line_kernel, S, T, C), out_shape=(jax.Sh...  155 us
    unnamed x7, local copies, waits for them, and re-layouts  4.5 us

profile of v2, /device:TPU:24, one launch (start us, length us, event | category | flops | bytes accessed | tf_op | source)
XLA Modules:
  0.0 160.1 jit_solution(14360947458124792347)
XLA Ops:
  0.6 155.0 %line.1 = (bf16[384,2048]{1,0:T(8,128)(2,1)}, bf16[2,2048,128]{2,1,0:T(8,128)(2,1)}, bf16[2,2,64,256]{3,2,1,0:T(8,128)(2,1)}) custom-call(s32[8]{0:T(128)} %counts.1, s32[8]{0:T(128)} %starts.1, s32[8]{0:T(128)} %owners.1, bf16[384,2048]{1,0:T(8,128)(2,1)} %x.1, bf16[384,2,1024]{2,1,0:T(2,128)(2,1)} %og.1, bf16[384,128]{1,0:T(8,128)(2,1)} %mid.1, ...), custom_call_target="tpu_custom_call" | custom-call | tf_op jit(solution)/shard_map/line/pallas_call | solution.py:633
  155.6 0.0 copy-start
  155.6 2.8 %copy.15 = bf16[384,2048]{1,0:T(8,128)(2,1)} copy(bf16[384,2048]{1,0:T(8,128)(2,1)} %get-tuple-element.6) | data formatting | bytes 3145728
  158.4 0.0 copy-done
  158.4 0.0 copy-start.1
  158.4 1.0 copy.16
  159.4 0.1 copy-done.1
  159.5 0.7 copy.17
Async XLA Ops:
  155.6 2.8 %copy-start = (bf16[2,2048,128]{2,1,0:T(8,128)(2,1)S(1)}, bf16[2,2048,128]{2,1,0:T(8,128)(2,1)}, u32[]{:S(2)}) copy-start(bf16[2,2048,128]{2,1,0:T(8,128)(2,1)} %get-tuple-element.7) | copy-start | bytes 3145732
  158.4 1.0 copy-start.1

commit v3 on v2

--- a/solution.py
+++ b/solution.py
@@ -176,9 +176,9 @@
 def line_kernel(
     S, T, C,
     counts, starts, owners,
-    x, og, mid, w_hbm, dn_hbm, up_hbm,
+    x_hbm, og_hbm, mid, w_hbm, dn_hbm, up_hbm,
     gi, gd, gu,
-    w, dn, up, low, gown, gright, gleft, mix, uown, uright, uleft, masked, lsel, msel,
+    x, og, w, dn, up, low, gown, gright, gleft, mix, uown, uright, uleft, masked, lsel, msel,
     copy_sem, up_s, up_r, low_s, low_r,
     w_s, w_r, y_s, y_r, dn_s, dn_r, g_s, g_r, u_s, u_r,
 ):
@@ -188,7 +188,7 @@
     c = lax.axis_index("sub")
     M = T * C
     m = t * C + c
-    rows, width = x.shape
+    rows, width = x_hbm.shape
     depth = w_hbm.shape[0]
     half = depth // 2
     piece = half // CHUNKS
@@ -216,7 +216,11 @@
         pltpu.make_async_copy(dn_hbm, dn.at[pl.ds(2 * s, 2)], copy_sem.at[1]),
         pltpu.make_async_copy(up_hbm, up.at[pl.ds(2 * s, 2)], copy_sem.at[2]),
     )
-    for cp in own:
+    late = (
+        pltpu.make_async_copy(og_hbm, og, copy_sem.at[3]),
+        pltpu.make_async_copy(x_hbm, x, copy_sem.at[4]),
+    )
+    for cp in own + late:
         cp.start()
 
     barrier = pltpu.get_barrier_semaphore()
@@ -370,6 +374,8 @@
             def _(p=p, j=j):
                 dn[2 * p + j] = jnp.zeros(dn.shape[1:], dn.dtype)
 
+    for cp in late:
+        cp.wait()
     slots = []
     for b in range(nblk):
         first = (s * nblk + b) * BLK
@@ -549,9 +555,11 @@
     for p in range(1, S - 1):
         grad_turn(0, p, True)
         grad_turn(1, S - 1 - p, True)
+    grad_turn(0, 1, False)
+    grad_turn(1, S - 2, False)
     for k in range(2, S - 1):
         hop(k)
-    for p in range(1, S - 1):
+    for p in range(2, S - 1):
         grad_turn(0, p, False)
         grad_turn(1, S - 1 - p, False)
     if S > 2:
@@ -637,9 +645,11 @@
             jax.ShapeDtypeStruct(adapter_down.shape, BF16),
             jax.ShapeDtypeStruct(adapter_up.shape, BF16),
         ),
-        in_specs=[smem] * 3 + [vmem] * 3 + [hbm] * 3,
+        in_specs=[smem] * 3 + [hbm] * 2 + [vmem] + [hbm] * 3,
         out_specs=(vmem, vmem, vmem),
         scratch_shapes=[
+            pltpu.VMEM((rows, width), BF16),
+            pltpu.VMEM(out_grad.shape, BF16),
             pltpu.VMEM((S * base_weight.shape[0], width), BF16),
             grads,
             ups,
@@ -650,7 +660,7 @@
             pltpu.VMEM((rows, kv2), BF16),
             pltpu.VMEM((rows, N * rank2), BF16),
             pltpu.VMEM((rows, N * rank2), BF16),
-            dma((3,)),
+            dma((5,)),
             dma((S - 1, 2)), dma((S - 1, 2)),
             dma((C + T,)), dma((C + T,)),
             dma((2, S - 1, CHUNKS)), dma((2, S - 1, CHUNKS)),

time: 160 us -> 159 us (level)
  no operation moved by 1% of the time
where the time goes in v3:
time: 159 us
  Pallas kernels  154 us (97%)
  local copies, waits for them, and re-layouts  4.5 us (3%)
    pallas_call x1, Pallas kernels, line_local(): pl.pallas_call(functools.partial(line_kernel, S, T, C), out_shape=(jax.Sh...  154 us
    unnamed x7, local copies, waits for them, and re-layouts  4.5 us

profile of v3, /device:TPU:24, one launch (start us, length us, event | category | flops | bytes accessed | tf_op | source)
XLA Modules:
  0.0 159.1 jit_solution(13942043082102380880)
XLA Ops:
  0.6 154.0 %line.1 = (bf16[384,2048]{1,0:T(8,128)(2,1)}, bf16[2,2048,128]{2,1,0:T(8,128)(2,1)}, bf16[2,2,64,256]{3,2,1,0:T(8,128)(2,1)}) custom-call(s32[8]{0:T(128)} %counts.1, s32[8]{0:T(128)} %starts.1, s32[8]{0:T(128)} %owners.1, bf16[384,2048]{1,0:T(8,128)(2,1)} %x_hbm.1, bf16[384,2,1024]{2,1,0:T(2,128)(2,1)} %og_hbm.1, bf16[384,128]{1,0:T(8,128)(2,1)} %mid.1, ...), custom_call_target="tpu_custom_call" | custom-call | tf_op jit(solution)/shard_map/line/pallas_call | solution.py:641
  154.6 0.0 copy-start
  154.6 2.8 %copy.15 = bf16[384,2048]{1,0:T(8,128)(2,1)} copy(bf16[384,2048]{1,0:T(8,128)(2,1)} %get-tuple-element.6) | data formatting | bytes 3145728
  157.5 0.0 copy-done
  157.5 0.0 copy-start.1
  157.5 1.0 copy.16
  158.4 0.1 copy-done.1
  158.5 0.7 copy.17
Async XLA Ops:
  154.6 2.8 %copy-start = (bf16[2,2048,128]{2,1,0:T(8,128)(2,1)S(1)}, bf16[2,2048,128]{2,1,0:T(8,128)(2,1)}, u32[]{:S(2)}) copy-start(bf16[2,2048,128]{2,1,0:T(8,128)(2,1)} %get-tuple-element.7) | copy-start | bytes 3145732
  157.5 1.0 copy-start.1
